TPU v7x, 128 devices: a whole 4x4x4 slice. The times are simulated.
128 devices in a mesh: dp: 16 (over x, z), centre: 8 (over y, core).
Axes of the slice: x: 4, y: 4, z: 4, core: 2. Of those that a mesh axis runs over, the one named last changes fastest.
Arguments:
- pool: bfloat16 [65536, 1024], P('dp'), may hold values from -6 to 6
- sample_idx: int32 [32768], P('dp'), may hold values from 0 to 4095
- assign: int32 [32768], P('dp'), may hold values from 0 to 31, as said below
- counts: int32 [32], P('centre'), may hold values from 256 to 2048
- old_centres: float32 [32, 1024], P('centre', 'dp'), may hold values from -6 to 6
- precond: bfloat16 [32, 1024, 1024], P('centre', 'dp'), may hold values from -1 to 1
Outputs:
- new_centres: float32 [32, 1024], P('centre', 'dp')
- row_loss: float32 [32768], P('dp')
Inputs may be any that keep to these rules, and one draw needn't show every extreme that they name: `assign`: in each aligned block of 2048 rows, no partition is named by more than 128 rows, and one partition, the same in every block, is named by exactly 128 rows.
All inputs are finite; a program needn't handle non-finite values.
Results may differ from a plain program's by a relative error of at most 0.0003.
Values may be sent and summed in bfloat16 or wider, within the bound.
A program may use at most 128 MiB of HBM per device.

v0:
```python
import math

import jax
import jax.numpy as jnp
from jax import lax
from jax.sharding import PartitionSpec as P

D = 1024
SWEEPS = 3


THRESHOLD = 0.4
EPSILON = 1e-06


def shards(pool, sample_idx, assign, counts, old_centres, precond):
    aniso = (D - 1) * THRESHOLD**2 / (1 - THRESHOLD**2)
    highest = lax.Precision.HIGHEST
    dp_count = lax.axis_size("dp")
    centre_count = lax.axis_size("centre")
    part_dev = counts.shape[0]
    row_dev = sample_idx.shape[0]
    slice_rows = D // dp_count
    offset = lax.axis_index("dp") * slice_rows
    first_part = lax.axis_index("centre") * part_dev
    mean_load = row_dev * dp_count / (part_dev * centre_count) * (D + aniso - 1.0) / D
    slab_rows = jnp.take(pool, sample_idx, axis=0)
    slab_float = slab_rows.astype(jnp.float32)
    inv_norm = lax.rsqrt(
        jnp.mean(slab_float * slab_float, axis=1, keepdims=True) + EPSILON
    ) / math.sqrt(D)
    unit_float = slab_float * inv_norm
    unit_rows = unit_float.astype(jnp.bfloat16)
    local_part = assign - first_part
    members = local_part[:, None] == jnp.arange(part_dev, dtype=jnp.int32)[None, :]
    member_low = members.astype(jnp.bfloat16)
    member_float = members.astype(jnp.float32)
    moment = aniso * jnp.dot(member_low.T, slab_rows, preferred_element_type=jnp.float32)
    row_ids = offset + jnp.arange(slice_rows, dtype=jnp.int32)
    eye_rows = (row_ids[:, None] == jnp.arange(D, dtype=jnp.int32)[None, :]).astype(jnp.float32)
    masked = member_low.T[:, :, None] * unit_rows[None, :, :]
    outer_sum = jnp.einsum("prd,re->pde", masked, unit_rows, preferred_element_type=jnp.float32)
    local_count = jnp.sum(member_float, axis=0)
    eye_full = jnp.eye(D, dtype=jnp.float32)
    partial_sum = (aniso - 1.0) * outer_sum + local_count[:, None, None] * eye_full[None, :, :]
    gram_rows, moment_rows = (
        lax.psum_scatter(partial_sum, "dp", scatter_dimension=1, tiled=True),
        lax.psum_scatter(moment, "dp", scatter_dimension=1, tiled=True),
    )
    prior = counts.astype(jnp.float32)
    gram_rows = gram_rows + prior[:, None, None] * eye_rows[None, :, :]
    moment_rows = moment_rows + prior[:, None] * old_centres
    diag_mean = prior + mean_load
    gram_norm = gram_rows / diag_mean[:, None, None]
    moment_norm = moment_rows / diag_mean[:, None]
    inverse = precond.astype(jnp.float32)

    def spread(row_part):
        return lax.all_gather(row_part, "dp", axis=1, tiled=True)

    def apply_inverse(row_part):
        return jnp.einsum("pij,pj->pi", inverse, spread(row_part), precision=highest)

    centre = apply_inverse(moment_norm)
    for sweep_step in range(SWEEPS):
        product = jnp.einsum("pij,pj->pi", gram_norm, spread(centre), precision=highest)
        centre = centre + apply_inverse(moment_norm - product)
    whole = spread(centre)
    chosen = jnp.dot(member_float, whole, precision=highest)
    deviation = slab_float - chosen
    along = jnp.sum(deviation * unit_float, axis=1)
    member_weight = jnp.sum(member_float, axis=1)
    local_loss = (
        member_weight
        * (jnp.sum(deviation * deviation, axis=1) + (aniso - 1.0) * along * along)
        / (aniso * D)
    )
    row_loss = lax.psum(local_loss, "centre")
    return (centre, row_loss)


def solution(mesh):
    return jax.shard_map(
        shards,
        mesh=mesh,
        in_specs=(
            P("dp", None),
            P("dp"),
            P("dp"),
            P("centre"),
            P("centre", "dp"),
            P("centre", "dp", None),
        ),
        out_specs=(P("centre", "dp"), P("dp")),
        check_vma=False,
    )
```

profile of v0, /device:TPU:1, one launch (start us, length us, event | category | flops | bytes accessed | tf_op | source)
XLA Modules:
  0.0 390.3 jit_solution(4545592186102533179)
XLA Ops:
  7.2 0.0 copy-start
  7.2 0.0 reduce-scatter.7.cloned.1.call-start
  7.2 0.8 fusion.37
  8.0 0.7 compare_and_fusion
  8.7 15.4 %gather_fusion = bf16[2048,1024]{1,0:T(8,128)(2,1)} fusion(bf16[4096,1024]{1,0:T(8,128)(2,1)} %param.6, s32[2048]{0:T(1024)S(1)} %fusion.37), kind=kCustom, calls=%fused_computation | custom fusion | bytes 8396800 | tf_op jit(solution)/shard_map/jit(_take)/gather | solution.py:27
  24.1 6.5 %copy.30 = bf16[2048,1024]{0,1:T(8,128)(2,1)} copy(bf16[2048,1024]{1,0:T(8,128)(2,1)} %gather_fusion) | data formatting | bytes 8388608 | tf_op jit(solution)/shard_map/jit(_take)/gather | solution.py:27
  30.6 3.4 fusion.14
  34.0 1.1 copy.56
  35.1 0.0 reduce-scatter.7.cloned.1.call-update
  35.1 0.0 reduce-scatter.5.cloned.1.call-start
  35.2 3.5 fusion.7
  38.6 0.1 convert_reduce_fusion
  38.8 0.5 fusion.11
  39.3 1.2 fusion.5
  40.5 21.8 %multiply_add_fusion = f32[4,1024,1024]{2,1,0:T(8,128)} fusion(f32[1024,1024]{1,0:T(8,128)S(1)} %fusion.11, f32[4]{0:T(128)S(1)} %get-tuple-element.5, bf16[2048,1024]{0,1:T(8,128)(2,1)S(1)} %fusion.5, bf16[4,2048]{1,0:T(4,128)(2,1)S(1)} %fusion.17), kind=kOutput, calls=%fused_computation.1 | convolution fusion | flops 17200840704 | bytes 25182224 | tf_op jit(solution)/shard_map/prd,re->pde/dot_general | solution.py:42
  62.4 0.0 reduce-scatter.5.cloned.1.call-update
  62.4 0.6 copy-done.5
  63.0 0.1 fusion.15
  63.1 46.2 %reduce-scatter.7.cloned.1.call-done = f32[64,4]{1,0:T(8,128)} async-done(((f32[1024,4]{1,0:T(8,128)}), f32[64,4]{1,0:T(8,128)}) %reduce-scatter.7.cloned.1.call-update) | async-done | bytes 1040
  109.3 0.8 copy.57
  110.1 0.1 add_divide_fusion.1
  110.2 16.9 %all-gather = f32[16,64,4]{1,2,0:T(4,128)S(1)} all-gather(f32[1,64,4]{1,2,0:T(4,128)S(1)} %bitcast.96), channel_id=1, replica_groups=mesh['dp'=16,'centre'=8] {'dp'}, dimensions={0}, use_global_device_ids=true | all-gather | bytes 17408 | tf_op jit(solution)/shard_map/all_gather | solution.py:59
  127.2 0.1 reshape.111
  127.2 0.5 fusion.30
  127.7 19.3 %all-gather.1 = f32[16,64,4]{1,2,0:T(4,128)S(1)} all-gather(f32[1,64,4]{1,2,0:T(4,128)S(1)} %bitcast.108), channel_id=1, replica_groups=mesh['dp'=16,'centre'=8] {'dp'}, dimensions={0}, use_global_device_ids=true | all-gather | bytes 17408 | tf_op jit(solution)/shard_map/all_gather | solution.py:59
  147.1 0.1 reshape.113
  147.2 77.4 %reduce-scatter.5.cloned.1.call-done = f32[4,64,1024]{2,1,0:T(8,128)} async-done(((f32[4,1024,1024]{2,1,0:T(8,128)}), f32[4,64,1024]{2,1,0:T(8,128)}) %reduce-scatter.5.cloned.1.call-update) | async-done | bytes 1048592 | tf_op jit(solution)/shard_map/reduce_scatter | solution.py:47
  224.6 1.4 add_divide_fusion
  226.0 1.0 fusion.28
  227.0 17.8 %all-gather.2 = f32[16,64,4]{1,2,0:T(4,128)S(1)} all-gather(f32[1,64,4]{1,2,0:T(4,128)S(1)} %subtract_bitcast_fusion.2), channel_id=1, replica_groups=mesh['dp'=16,'centre'=8] {'dp'}, dimensions={0}, use_global_device_ids=true | all-gather | bytes 17408 | tf_op jit(solution)/shard_map/all_gather | solution.py:59
  244.9 0.1 reshape.115
  245.0 0.5 fusion.26
  245.5 15.9 %all-gather.3 = f32[16,64,4]{1,2,0:T(4,128)S(1)} all-gather(f32[1,64,4]{1,2,0:T(4,128)S(1)} %bitcast.99), channel_id=1, replica_groups=mesh['dp'=16,'centre'=8] {'dp'}, dimensions={0}, use_global_device_ids=true | all-gather | bytes 17408 | tf_op jit(solution)/shard_map/all_gather | solution.py:59
  261.4 0.1 reshape.117
  261.4 1.0 fusion.24
  262.4 17.0 %all-gather.4 = f32[16,64,4]{1,2,0:T(4,128)S(1)} all-gather(f32[1,64,4]{1,2,0:T(4,128)S(1)} %subtract_bitcast_fusion.1), channel_id=1, replica_groups=mesh['dp'=16,'centre'=8] {'dp'}, dimensions={0}, use_global_device_ids=true | all-gather | bytes 17408 | tf_op jit(solution)/shard_map/all_gather | solution.py:59
  279.4 0.1 reshape.119
  279.5 0.5 fusion.22
  280.0 16.2 %all-gather.5 = f32[16,64,4]{1,2,0:T(4,128)S(1)} all-gather(f32[1,64,4]{1,2,0:T(4,128)S(1)} %bitcast.98), channel_id=1, replica_groups=mesh['dp'=16,'centre'=8] {'dp'}, dimensions={0}, use_global_device_ids=true | all-gather | bytes 17408 | tf_op jit(solution)/shard_map/all_gather | solution.py:59
  296.2 0.1 reshape.121
  296.3 1.0 fusion.20
  297.3 16.5 %all-gather.6 = f32[16,64,4]{1,2,0:T(4,128)S(1)} all-gather(f32[1,64,4]{1,2,0:T(4,128)S(1)} %subtract_bitcast_fusion), channel_id=1, replica_groups=mesh['dp'=16,'centre'=8] {'dp'}, dimensions={0}, use_global_device_ids=true | all-gather | bytes 17408 | tf_op jit(solution)/shard_map/all_gather | solution.py:59
  313.8 0.1 reshape.123
  313.9 0.5 fusion.18
  314.4 16.2 %all-gather.7 = f32[16,64,4]{1,2,0:T(4,128)S(1)} all-gather(f32[1,64,4]{1,2,0:T(4,128)S(1)} %bitcast.107), channel_id=1, replica_groups=mesh['dp'=16,'centre'=8] {'dp'}, dimensions={0}, use_global_device_ids=true | all-gather | bytes 17408 | tf_op jit(solution)/shard_map/all_gather | solution.py:59
  330.7 0.1 reshape.125
  330.8 7.3 %fusion.6 = (f32[2048]{0:T(1024)S(1)}, f32[2048]{0:T(1024)S(1)}) fusion(f32[2048]{0:T(1024)S(1)} %rsqrt_multiply_fusion, bf16[2048,1024]{0,1:T(8,128)(2,1)} %copy.30, pred[2048]{0:T(1024)(128)(4,1)S(1)} %compare_and_fusion, f32[1024,4]{0,1:T(4,128)S(1)} %reshape.125, s32[2048]{0:T(1024)S(1)} %broadcast_subtract_fusion), kind=kOutput, calls=%fused_computation.9 | convolution fusion | flops 117444608 | bytes 4245504 | tf_op jit(solution)/shard_map/dot_general | solution.py:69
  338.1 45.4 %psum.7 = f32[2048]{0:T(1024)} all-reduce(f32[2048]{0:T(1024)S(1)} %fusion.36), channel_id=1, replica_groups=mesh['dp'=16,'centre'=8] {'centre'}, use_global_device_ids=true, to_apply=%region_7.8 | all-reduce | flops 2048 | bytes 16384 | tf_op jit(solution)/shard_map/psum | solution.py:78
  (31 shorter events, 0.1 us)
Async XLA Ops:
  7.2 120.1 %copy-start = (bf16[4,64,1024]{2,1,0:T(8,128)(2,1)S(1)}, bf16[4,64,1024]{2,1,0:T(8,128)(2,1)}, u32[]{:S(2)}) copy-start(bf16[4,64,1024]{2,1,0:T(8,128)(2,1)} %param.11) | copy-start | bytes 1572868
  7.2 102.1 %reduce-scatter.7.cloned.1.call-start = ((), (), s32[]{:S(2)}) async-start(), calls=%async_computation.3 | async-start | bytes 557056
  24.1 6.5 %copy-start.3 = (s32[2048]{0:T(1024)S(1)}, s32[2048]{0:T(1024)}, u32[]{:S(2)}) copy-start(s32[2048]{0:T(1024)} %param.8) | copy-start | bytes 24580
  35.1 189.5 %reduce-scatter.5.cloned.1.call-start = ((), (), s32[]{:S(2)}) async-start(), calls=%async_computation.2 | async-start | bytes 17825792 | tf_op jit(solution)/shard_map/reduce_scatter | solution.py:47
  35.1 4.2 %copy-start.1 = (bf16[2048,1024]{0,1:T(8,128)(2,1)S(1)}, bf16[2048,1024]{0,1:T(8,128)(2,1)}, u32[]{:S(2)}) copy-start(bf16[2048,1024]{0,1:T(8,128)(2,1)} %copy.30) | copy-start | bytes 12582916
  62.4 0.7 copy-start.5
  62.4 47.8 %copy-start.4 = (f32[4,64]{1,0:T(4,128)S(1)}, f32[4,64]{1,0:T(4,128)}, u32[]{:S(2)}) copy-start(f32[4,64]{1,0:T(4,128)} %param.10) | copy-start | bytes 3076
  314.4 23.6 %copy-start.2 = (f32[4,64]{1,0:T(4,128)}, f32[4,64]{1,0:T(4,128)S(1)}, u32[]{:S(2)}) copy-start(f32[4,64]{1,0:T(4,128)S(1)} %add.71) | copy-start | bytes 3076
Sparse Core Ops, SparseCore 0:
  35.2 74.0 reduce-scatter.6
  113.1 111.4 reduce-scatter.4
where the time goes:
time: 391 us; the launch traced here: 390 us
  blocking collectives  181 us (46%)
  waiting for transfers between devices  124 us (32%)
  matrix products  37.5 us (10%)
  local copies, waits for them, and re-layouts  25.2 us (6%)
  between operations  14.2 us (4%)
  other arithmetic  8.47 us (2%)
    all_gather x8, blocking collectives, spread(): return lax.all_gather(row_part, 'dp', axis=1, tiled=True)  136 us
    reduce_scatter x1, waiting for transfers between devices, shards(): lax.psum_scatter(partial_sum, 'dp', scatter_dimension=1, tiled=True)  77.4 us
    unnamed x3, waiting for transfers between devices  46.2 us
    psum x1, blocking collectives, shards(): row_loss = lax.psum(local_loss, 'centre')  45.4 us
    gather x2, local copies, waits for them, and re-layouts, shards(): slab_rows = jnp.take(pool, sample_idx, axis=0)  21.9 us
    dot_general x1, matrix products, shards(): jnp.einsum('prd,re->pde', masked, unit_rows, preferred_element_type=jnp.f...  21.8 us
  transfers between devices with their start and end apart: 2, of which 2 were waited for; matrix products, arithmetic and copies ran while one was open for 7% of the time, Pallas kernels for 0%

commit v1 on v0

v1 whole, which is shorter than its diff:
```python
import functools
import math

import jax
import jax.numpy as jnp
from jax import lax
from jax.experimental import pallas as pl
from jax.experimental.pallas import tpu as pltpu
from jax.sharding import PartitionSpec as P

D = 1024
SWEEPS = 3
CAP = 128
THRESHOLD = 0.4
EPSILON = 1e-06
ANISO = (D - 1) * THRESHOLD**2 / (1 - THRESHOLD**2)

LANES = 128
CHUNKS = D // LANES
SIDE = 4
COLS = 256
STEPS = D // COLS
MESH = pl.DeviceIdType.MESH


def iota(shape, axis):
    return lax.broadcasted_iota(jnp.int32, shape, axis)


def kernel(
    centre_count,
    mean_load,
    sample_ref,
    assign_ref,
    counts_ref,
    old_ref,
    precond_ref,
    pool_ref,
    centres_ref,
    loss_ref,
    pool_buf,
    picker,
    slot_of,
    picked,
    rows_in,
    unit,
    inv_own,
    inverse,
    moment_out,
    moment_in,
    line_out,
    line_in,
    whole_out,
    whole_in,
    loss_out,
    loss_in,
    pool_sem,
    own_sem,
    inv_send,
    inv_recv,
    row_send,
    row_recv,
    moment_sem,
    line_send,
    line_recv,
    whole_sem,
    loss_sem,
):
    place = lax.axis_index("dp")
    centre = lax.axis_index("centre")
    core = lax.rem(centre, 2)
    px, pz = place // SIDE, lax.rem(place, SIDE)
    group = (1 - core) * pz + core * px
    member = (1 - core) * px + core * pz

    def device(a, b):
        m, k = lax.rem(member + a, SIDE), lax.rem(group + b, SIDE)
        return (1 - core) * (m * SIDE + k) + core * (k * SIDE + m)

    def partition(b):
        return lax.rem(group + b, SIDE)

    def pool_copy(q):
        return pltpu.make_async_copy(
            pool_ref.at[:, pl.ds(q * COLS, COLS)], pool_buf.at[q], pool_sem.at[q]
        )

    for q in range(STEPS):
        pool_copy(q).start()
    own_inverse = pltpu.make_async_copy(precond_ref.at[group], inverse.at[0], own_sem)
    own_inverse.start()

    barrier = pltpu.get_barrier_semaphore()
    for a in range(SIDE):
        for b in range(SIDE):
            if a or b:
                pl.semaphore_signal(barrier, inc=1, device_id=(device(a, b), centre), device_id_type=MESH)
    for k in range(1, centre_count):
        pl.semaphore_signal(
            barrier, inc=1, device_id=(place, lax.rem(centre + k, centre_count)), device_id_type=MESH
        )

    first = centre * SIDE
    assign = assign_ref[...]
    masks = [(assign == first + k) for k in range(SIDE)]
    mask_all = jnp.concatenate([m.astype(jnp.float32) for m in masks], axis=0).astype(jnp.bfloat16)
    lane_row, lane_col = iota((LANES, LANES), 0), iota((LANES, LANES), 1)
    upper = (lane_row <= lane_col).astype(jnp.float32).astype(jnp.bfloat16)
    inside = jnp.dot(mask_all, upper, preferred_element_type=jnp.float32)
    ones = jnp.ones((LANES, LANES), jnp.bfloat16)
    totals = jnp.dot(mask_all, ones, preferred_element_type=jnp.float32)
    span = assign.shape[0]
    big_row, big_col = iota((SIDE * span, SIDE * span), 0), iota((SIDE * span, SIDE * span), 1)
    same = (big_row // span) == (big_col // span)
    before = (same & (big_col < big_row)).astype(jnp.float32).astype(jnp.bfloat16)
    ahead = jnp.dot(before, totals.astype(jnp.bfloat16), preferred_element_type=jnp.float32)
    rank = (inside + ahead).astype(jnp.int32) - 1
    for k in range(SIDE):
        slot_of[k * span : (k + 1) * span, :] = jnp.where(masks[k], rank[k * span : (k + 1) * span, :], -1)
    named = [jnp.sum(totals[k * span : (k + 1) * span, :], axis=0, keepdims=True) for k in range(SIDE)]

    sample = sample_ref[...] + 1
    slot_row = iota((CAP, LANES), 0)
    for k in range(SIDE):
        total = jnp.zeros((CAP, LANES), jnp.int32)
        for r in range(span):
            hit = slot_of[k * span + r : k * span + r + 1, :] == slot_row
            total += jnp.where(hit, sample[r : r + 1, :], 0)
        index = jnp.sum(total.astype(jnp.float32), axis=1, keepdims=True).astype(jnp.int32) - 1

        def pick(t, carry):
            hot = (iota((CAP, COLS), 1) + t * COLS) == index
            picker[t, k * CAP : (k + 1) * CAP, :] = hot.astype(jnp.float32).astype(jnp.bfloat16)
            return carry

        lax.fori_loop(0, picker.shape[0], pick, 0)

    pl.semaphore_wait(barrier, SIDE * SIDE - 1 + centre_count - 1)
    inverse_copies = []
    for b in range(1, SIDE):
        copy = pltpu.make_async_remote_copy(
            src_ref=precond_ref.at[partition(b)],
            dst_ref=inverse.at[b],
            send_sem=inv_send.at[b],
            recv_sem=inv_recv.at[b],
            device_id=(device(0, b), centre),
            device_id_type=MESH,
        )
        copy.start()
        inverse_copies.append(copy)

    sums = []
    row_copies = []
    for q in range(STEPS):
        pool_copy(q).wait()

        block = jnp.zeros((SIDE * CAP, COLS), jnp.float32)
        for t in range(picker.shape[0]):
            block += jnp.dot(
                picker[t], pool_buf[q, t * COLS : (t + 1) * COLS, :], preferred_element_type=jnp.float32
            )
        picked[q] = block.astype(jnp.bfloat16)
        sums.append(
            [jnp.sum(block[k * CAP : (k + 1) * CAP, :], axis=0, keepdims=True) for k in range(SIDE)]
        )
        for b in range(1, SIDE):
            copy = pltpu.make_async_remote_copy(
                src_ref=picked.at[q, pl.ds(partition(b) * CAP, CAP)],
                dst_ref=rows_in.at[b, q],
                send_sem=row_send.at[b, q],
                recv_sem=row_recv.at[b, q],
                device_id=(device(0, b), centre),
                device_id_type=MESH,
            )
            copy.start()
            row_copies.append(copy)

    tile_row = iota((CHUNKS, LANES), 0)
    half = lax.rem(place, 2)
    old = old_ref[...]
    twice = jnp.concatenate([old, old], axis=1)
    twice = jnp.where(iota(twice.shape, 1) // (LANES // 2) == half, twice, 0.0)
    for k in range(SIDE):
        rows = []
        for q in range(STEPS):
            for s in range(COLS // LANES):
                rows.append(sums[q][k][:, s * LANES : (s + 1) * LANES])
        tile = ANISO * jnp.concatenate(rows, axis=0)
        prior = counts_ref[k].astype(jnp.float32)
        tile += jnp.where(tile_row == place // 2, prior * twice[k : k + 1, :], 0.0)
        moment_out[k, 0] = tile
        moment_out[k, 1] = jnp.broadcast_to(named[k], (CHUNKS, LANES))
    for a in range(SIDE):
        for b in range(SIDE):
            if a or b:
                pltpu.make_async_remote_copy(
                    src_ref=moment_out.at[partition(b)],
                    dst_ref=moment_in.at[a * SIDE + b],
                    send_sem=moment_sem.at[0],
                    recv_sem=moment_sem.at[1],
                    device_id=(device(a, b), centre),
                    device_id_type=MESH,
                ).start()

    def own_norm(i, carry):
        rows = pl.ds(i * 32, 32)
        total = jnp.zeros((32, COLS), jnp.float32)
        for q in range(STEPS):
            x = picked[q, rows, :].astype(jnp.float32)
            total += x * x
        mean = jnp.sum(total, axis=1, keepdims=True) * (1.0 / D)
        inv_own[rows, :] = jnp.broadcast_to(lax.rsqrt(mean + EPSILON) / math.sqrt(D), (32, LANES))
        return carry

    lax.fori_loop(0, SIDE * CAP // 32, own_norm, 0)

    own_inverse.wait()
    for copy in inverse_copies:
        copy.wait_recv()
    arrived = moment_in.at[pl.ds(1, SIDE * SIDE - 1)]
    pltpu.make_async_copy(arrived, arrived, moment_sem.at[1]).wait()
    moment = moment_out[group, 0]
    count = moment_out[group, 1]
    for s in range(1, SIDE * SIDE):
        moment += moment_in[s, 0]
        count += moment_in[s, 1]
    prior = counts_ref[group].astype(jnp.float32)
    scale = prior + mean_load
    moment = moment / scale
    ridge = (count + prior) / scale

    block_row, block_lane = iota((64, LANES), 0), iota((64, LANES), 1)

    def apply_inverse(vector):
        tile = jnp.zeros((CHUNKS, LANES), jnp.float32)
        for b in range(SIDE):
            total = jnp.zeros((64, LANES), jnp.float32)
            for r in range(CHUNKS):
                w = inverse[b, :, r * LANES : (r + 1) * LANES].astype(jnp.float32)
                total += w * vector[r : r + 1, :]
            column = jnp.sum(total, axis=1, keepdims=True)
            home = device(0, SIDE - b)
            spread = jnp.where(block_lane == block_row + 64 * lax.rem(home, 2), column, 0.0)
            spread = jnp.sum(spread, axis=0, keepdims=True)
            tile += jnp.where(tile_row == home // 2, spread, 0.0)
        return tile

    def apply_outer(vector):
        def step(i, carry):
            rows = pl.ds(i * 32, 32)
            total = jnp.zeros((32, LANES), jnp.float32)
            pieces = []
            for r in range(CHUNKS):
                u = unit[rows, r * LANES : (r + 1) * LANES]
                pieces.append(u)
                total += u * vector[r : r + 1, :]
            along = jnp.sum(total, axis=1, keepdims=True)
            out = []
            for r in range(CHUNKS):
                v = pieces[r] * along
                out.append(carry[r] + ((v[0:8] + v[8:16]) + (v[16:24] + v[24:32])))
            return tuple(out)

        zero = tuple(jnp.zeros((8, LANES), jnp.float32) for _ in range(CHUNKS))
        parts = lax.fori_loop(0, SIDE * CAP // 32, step, zero, unroll=4)
        return jnp.concatenate([jnp.sum(p, axis=0, keepdims=True) for p in parts], axis=0)

    def line_sum(turn, tile):
        line_out[turn] = tile
        for a in range(1, SIDE):
            pltpu.make_async_remote_copy(
                src_ref=line_out.at[turn],
                dst_ref=line_in.at[turn, a],
                send_sem=line_send.at[turn],
                recv_sem=line_recv.at[turn],
                device_id=(device(a, 0), centre),
                device_id_type=MESH,
            ).start()
        here = line_in.at[turn, pl.ds(1, SIDE - 1)]

        def finish():
            pltpu.make_async_copy(here, here, line_recv.at[turn]).wait()
            return (tile + line_in[turn, 1]) + (line_in[turn, 2] + line_in[turn, 3])

        return finish

    finish = line_sum(0, apply_inverse(moment))

    for b in range(SIDE):
        if b:
            for q in range(STEPS):
                pltpu.make_async_copy(rows_in.at[b, q], rows_in.at[b, q], row_recv.at[b, q]).wait()

        def normalise(i, carry):
            x = []
            for q in range(STEPS):
                if b:
                    x.append(rows_in[b, q, pl.ds(i * 32, 32), :].astype(jnp.float32))
                else:
                    x.append(picked[q, pl.ds(group * CAP + i * 32, 32), :].astype(jnp.float32))
            total = jnp.zeros((32, COLS), jnp.float32)
            for q in range(STEPS):
                total += x[q] * x[q]
            mean = jnp.sum(total, axis=1, keepdims=True) * (1.0 / D)
            inv = lax.rsqrt(mean + EPSILON) / math.sqrt(D)
            for q in range(STEPS):
                u = (x[q] * inv).astype(jnp.bfloat16).astype(jnp.float32)
                unit[pl.ds(b * CAP + i * 32, 32), q * COLS : (q + 1) * COLS] = u
            return carry

        lax.fori_loop(0, CAP // 32, normalise, 0)

    vector = finish()
    for sweep in range(SWEEPS):
        product = line_sum(2 * sweep + 1, apply_outer(vector))()
        slack = moment - ((ANISO - 1.0) / scale * product + ridge * vector)
        change = apply_inverse(slack)
        if sweep < SWEEPS - 1:
            vector = vector + line_sum(2 * sweep + 2, change)()

    lane = iota((CHUNKS, LANES), 1)
    mine = jnp.zeros((CHUNKS, LANES), jnp.float32)
    for b in range(SIDE):
        home = device(0, b)
        mine += jnp.where((tile_row == home // 2) & (lane // 64 == lax.rem(home, 2)), vector, 0.0)
    whole_out[...] = mine + change
    for a in range(SIDE):
        for b in range(SIDE):
            if a or b:
                pltpu.make_async_remote_copy(
                    src_ref=whole_out,
                    dst_ref=whole_in.at[a * SIDE + b],
                    send_sem=whole_sem.at[0],
                    recv_sem=whole_sem.at[1],
                    device_id=(device(a, b), centre),
                    device_id_type=MESH,
                ).start()
    arrived = whole_in.at[pl.ds(1, SIDE * SIDE - 1)]
    pltpu.make_async_copy(arrived, arrived, whole_sem.at[1]).wait()

    losses = jnp.zeros((span, LANES), jnp.float32)
    centres = jnp.zeros((SIDE, LANES), jnp.float32)
    part_row = iota((SIDE, LANES), 0)
    span_row = iota((span, LANES), 0)
    for b in range(SIDE):
        k = lax.rem(group + SIDE - b, SIDE)
        tile = whole_out[...] if b == 0 else whole_in[b]
        for a in range(1, SIDE):
            tile = tile + whole_in[a * SIDE + b]
        block = jnp.sum(jnp.where(tile_row == place // 2, tile, 0.0), axis=0, keepdims=True)
        centres += jnp.where(part_row == k, block, 0.0)

        columns = []
        for i in range(CAP // 32):
            rows = pl.ds(k * CAP + i * 32, 32)
            square = jnp.zeros((32, LANES), jnp.float32)
            along = jnp.zeros((32, LANES), jnp.float32)
            for q in range(STEPS):
                x = picked[q, rows, :].astype(jnp.float32)
                for s in range(COLS // LANES):
                    r = q * (COLS // LANES) + s
                    xs = x[:, s * LANES : (s + 1) * LANES]
                    deviation = xs - tile[r : r + 1, :]
                    square += deviation * deviation
                    along += deviation * xs
            along = jnp.sum(along, axis=1, keepdims=True) * inv_own[rows, 0:1]
            square = jnp.sum(square, axis=1, keepdims=True)
            columns.append((square + (ANISO - 1.0) * along * along) / (ANISO * D))
        column = jnp.concatenate(columns, axis=0)
        slots = slot_of[pl.ds(k * span, span), :]
        for r in range(span):
            hit = slots[r : r + 1, :] == slot_row
            row = jnp.sum(jnp.where(hit, column, 0.0), axis=0, keepdims=True)
            losses += jnp.where(span_row == r, row, 0.0)

    loss_out[...] = losses
    for k in range(1, centre_count):
        pltpu.make_async_remote_copy(
            src_ref=loss_out,
            dst_ref=loss_in.at[k],
            send_sem=loss_sem.at[0],
            recv_sem=loss_sem.at[1],
            device_id=(place, lax.rem(centre + k, centre_count)),
            device_id_type=MESH,
        ).start()

    swapped = jnp.concatenate([centres[:, 64:], centres[:, :64]], axis=1)
    centres_ref[...] = jnp.where(half == 0, centres, swapped)[:, :64]
    for copy in inverse_copies + row_copies:
        copy.wait_send()
    sent = moment_in.at[pl.ds(1, SIDE * SIDE - 1)]
    pltpu.make_async_copy(sent, sent, moment_sem.at[0]).wait()
    for turn in range(2 * SWEEPS):
        sent = line_in.at[turn, pl.ds(1, SIDE - 1)]
        pltpu.make_async_copy(sent, sent, line_send.at[turn]).wait()
    sent = whole_in.at[pl.ds(1, SIDE * SIDE - 1)]
    pltpu.make_async_copy(sent, sent, whole_sem.at[0]).wait()
    if centre_count > 1:
        arrived = loss_in.at[pl.ds(1, centre_count - 1)]
        pltpu.make_async_copy(arrived, arrived, loss_sem.at[1]).wait()
        for k in range(1, centre_count):
            losses = losses + loss_in[k]
        pltpu.make_async_copy(arrived, arrived, loss_sem.at[0]).wait()
    loss_ref[...] = losses


def shards(pool, sample_idx, assign, counts, old_centres, precond):
    centre_count = lax.axis_size("centre")
    dp_count = lax.axis_size("dp")
    row_dev = sample_idx.shape[0]
    span = row_dev // LANES
    part_dev = counts.shape[0]
    mean_load = row_dev * dp_count / (part_dev * centre_count) * (D + ANISO - 1.0) / D
    pool_rows = pool.shape[0]
    f32, bf16 = jnp.float32, jnp.bfloat16
    vmem = pl.BlockSpec(memory_space=pltpu.VMEM)
    dma = pltpu.SemaphoreType.DMA
    plane = SIDE * SIDE
    centres, loss = pl.pallas_call(
        functools.partial(kernel, centre_count, mean_load),
        out_shape=(
            jax.ShapeDtypeStruct((part_dev, D // dp_count), f32),
            jax.ShapeDtypeStruct((span, LANES), f32),
        ),
        in_specs=[
            vmem,
            vmem,
            pl.BlockSpec(memory_space=pltpu.SMEM),
            vmem,
            pl.BlockSpec(memory_space=pl.ANY),
            pl.BlockSpec(memory_space=pl.ANY),
        ],
        out_specs=(vmem, vmem),
        scratch_shapes=[
            pltpu.VMEM((STEPS, pool_rows, COLS), bf16),
            pltpu.VMEM((pool_rows // COLS, SIDE * CAP, COLS), bf16),
            pltpu.VMEM((SIDE * span, LANES), jnp.int32),
            pltpu.VMEM((STEPS, SIDE * CAP, COLS), bf16),
            pltpu.VMEM((SIDE, STEPS, CAP, COLS), bf16),
            pltpu.VMEM((SIDE * CAP, D), f32),
            pltpu.VMEM((SIDE * CAP, LANES), f32),
            pltpu.VMEM((SIDE, D // dp_count, D), bf16),
            pltpu.VMEM((SIDE, 2, CHUNKS, LANES), f32),
            pltpu.VMEM((plane, 2, CHUNKS, LANES), f32),
            pltpu.VMEM((2 * SWEEPS, CHUNKS, LANES), f32),
            pltpu.VMEM((2 * SWEEPS, SIDE, CHUNKS, LANES), f32),
            pltpu.VMEM((CHUNKS, LANES), f32),
            pltpu.VMEM((plane, CHUNKS, LANES), f32),
            pltpu.VMEM((span, LANES), f32),
            pltpu.VMEM((centre_count, span, LANES), f32),
            dma((STEPS,)),
            dma,
            dma((SIDE,)),
            dma((SIDE,)),
            dma((SIDE, STEPS)),
            dma((SIDE, STEPS)),
            dma((2,)),
            dma((2 * SWEEPS,)),
            dma((2 * SWEEPS,)),
            dma((2,)),
            dma((2,)),
        ],
        compiler_params=pltpu.CompilerParams(
            collective_id=0, has_side_effects=True, vmem_limit_bytes=48 * 1024 * 1024
        ),
    )(sample_idx.reshape(span, LANES), assign.reshape(span, LANES), counts, old_centres, precond, pool)
    return centres, loss.reshape(row_dev)


def solution(mesh):
    return jax.shard_map(
        shards,
        mesh=mesh,
        in_specs=(
            P("dp", None),
            P("dp"),
            P("dp"),
            P("centre"),
            P("centre", "dp"),
            P("centre", "dp", None),
        ),
        out_specs=(P("centre", "dp"), P("dp")),
        check_vma=False,
    )
```

time: 391 us -> 63.8 us (0.16)
  blocking collectives: 181 us -> 0 us
  waiting for transfers between devices: 124 us -> 0 us
  Pallas kernels: 0 us -> 57.9 us
  matrix products: 37.5 us -> 0 us
  local copies, waits for them, and re-layouts: 25.2 us -> 4.94 us
  between operations: 14.2 us -> 0.65 us
  other arithmetic: 8.47 us -> 0 us
    all_gather x8 -> x0, blocking collectives: 136 us -> none  [spread(): return lax.all_gather(row_part, 'dp', axis=1, tiled=True)]
    reduce_scatter x1 -> x0, waiting for transfers between devices: 77.4 us -> none  [shards(): lax.psum_scatter(partial_sum, 'dp', scatter_dimension=1, tiled=True)]
    pallas_call x0 -> x1, Pallas kernels: none -> 57.9 us  [shards(): pl.pallas_call(functools.partial(kernel, centre_count, mean_load), out_sh...]
    unnamed x3 -> x0, waiting for transfers between devices: 46.2 us -> none
    psum x1 -> x0, blocking collectives: 45.4 us -> none  [shards(): row_loss = lax.psum(local_loss, 'centre')]
    dot_general x10 -> x0, matrix products: 37.5 us -> none  [the longest x1 21.8 us: shards(): jnp.einsum('prd,re->pde', masked, unit_rows, preferred_element_type=jnp.f...]
    gather x2 -> x0, local copies, waits for them, and re-layouts: 21.9 us -> none  [shards(): slab_rows = jnp.take(pool, sample_idx, axis=0)]
  transfers between devices with their start and end apart: 2 -> 0, of which waited for: 2 -> 0; matrix products, arithmetic and copies ran while one was open for 7% -> 0% of each run, Pallas kernels for 0% -> 0%
where the time goes in v1:
time: 63.8 us; the launch traced here: 63.5 us
  Pallas kernels  57.9 us (91%)
  local copies, waits for them, and re-layouts  4.94 us (8%)
  between operations  0.65 us (1%)
    pallas_call x1, Pallas kernels, shards(): pl.pallas_call(functools.partial(kernel, centre_count, mean_load), out_sh...  57.9 us
    unnamed x12, local copies, waits for them, and re-layouts  4.94 us

profile of v1, /device:TPU:1, one launch (start us, length us, event | category | flops | bytes accessed | tf_op | source)
XLA Modules:
  0.0 63.5 jit_solution(340249529130167467)
XLA Ops:
  0.6 0.0 copy-start
  0.6 1.0 %copy-done = bf16[4,64,1024]{2,1,0:T(8,128)(2,1)S(1)} copy-done((bf16[4,64,1024]{2,1,0:T(8,128)(2,1)S(1)}, bf16[4,64,1024]{2,1,0:T(8,128)(2,1)}, u32[]{:S(2)}) %copy-start) | copy-done | bytes 524312
  1.7 0.0 copy-start.1
  1.7 0.7 %copy-done.1 = s32[2048]{0:T(1024)S(1)} copy-done((s32[2048]{0:T(1024)S(1)}, s32[2048]{0:T(1024)}, u32[]{:S(2)}) %copy-start.1) | copy-done | bytes 8216
  2.4 0.0 copy-start.2
  2.4 0.7 %copy-done.2 = s32[2048]{0:T(1024)S(1)} copy-done((s32[2048]{0:T(1024)S(1)}, s32[2048]{0:T(1024)}, u32[]{:S(2)}) %copy-start.2) | copy-done | bytes 8216
  3.1 0.0 copy-start.3
  3.1 0.7 %copy-done.3 = f32[4,64]{1,0:T(4,128)S(1)} copy-done((f32[4,64]{1,0:T(4,128)S(1)}, f32[4,64]{1,0:T(4,128)}, u32[]{:S(2)}) %copy-start.3) | copy-done | bytes 1048
  3.8 0.0 copy-start.4
  3.8 0.7 %copy-done.4 = s32[4]{0:T(128)S(1)} copy-done((s32[4]{0:T(128)S(1)}, s32[4]{0:T(128)}, u32[]{:S(2)}) %copy-start.4) | copy-done | bytes 40
  4.4 57.9 %shard_map.77 = (f32[4,64]{1,0:T(4,128)S(1)}, f32[16,128]{1,0:T(8,128)S(1)}) custom-call(s32[16,128]{1,0:T(8,128)S(1)} %bitcast.3, s32[16,128]{1,0:T(8,128)S(1)} %bitcast.4, s32[4]{0:T(128)S(1)} %copy-done.4, f32[4,64]{1,0:T(4,128)S(1)} %copy-done.3, bf16[4,64,1024]{2,1,0:T(8,128)(2,1)S(1)} %copy-done, bf16[4096,1024]{1,0:T(8,128)(2,1)} %pool_ref.1), custom_call_target="tpu_custom_call" | custom-call | tf_op jit(solution)/shard_map/pallas_call | solution.py:419
  62.3 0.6 copy.10
  62.9 0.6 copy.11
Async XLA Ops:
  0.6 1.0 %copy-start = (bf16[4,64,1024]{2,1,0:T(8,128)(2,1)S(1)}, bf16[4,64,1024]{2,1,0:T(8,128)(2,1)}, u32[]{:S(2)}) copy-start(bf16[4,64,1024]{2,1,0:T(8,128)(2,1)} %precond_ref.1) | copy-start | bytes 1572868
  1.7 0.7 %copy-start.1 = (s32[2048]{0:T(1024)S(1)}, s32[2048]{0:T(1024)}, u32[]{:S(2)}) copy-start(s32[2048]{0:T(1024)} %param.7) | copy-start | bytes 24580
  2.4 0.7 %copy-start.2 = (s32[2048]{0:T(1024)S(1)}, s32[2048]{0:T(1024)}, u32[]{:S(2)}) copy-start(s32[2048]{0:T(1024)} %param.8) | copy-start | bytes 24580
  3.1 0.7 %copy-start.3 = (f32[4,64]{1,0:T(4,128)S(1)}, f32[4,64]{1,0:T(4,128)}, u32[]{:S(2)}) copy-start(f32[4,64]{1,0:T(4,128)} %old_ref.1) | copy-start | bytes 3076
  3.8 0.7 %copy-start.4 = (s32[4]{0:T(128)S(1)}, s32[4]{0:T(128)}, u32[]{:S(2)}) copy-start(s32[4]{0:T(128)} %counts_ref.1) | copy-start | bytes 52

commit v2 on v1

--- a/solution.py
+++ b/solution.py
@@ -18,8 +18,7 @@
 LANES = 128
 CHUNKS = D // LANES
 SIDE = 4
-COLS = 256
-STEPS = D // COLS
+PIECES = 8
 MESH = pl.DeviceIdType.MESH
 
 
@@ -30,14 +29,18 @@
 def kernel(
     centre_count,
     mean_load,
+    sample_hbm,
+    assign_hbm,
+    counts_hbm,
+    old_hbm,
+    precond_ref,
+    pool_ref,
+    centres_ref,
+    loss_ref,
     sample_ref,
     assign_ref,
     counts_ref,
     old_ref,
-    precond_ref,
-    pool_ref,
-    centres_ref,
-    loss_ref,
     pool_buf,
     picker,
     slot_of,
@@ -54,6 +57,7 @@
     whole_in,
     loss_out,
     loss_in,
+    small_sem,
     pool_sem,
     own_sem,
     inv_send,
@@ -81,11 +85,18 @@
         return lax.rem(group + b, SIDE)
 
     def pool_copy(q):
-        return pltpu.make_async_copy(
-            pool_ref.at[:, pl.ds(q * COLS, COLS)], pool_buf.at[q], pool_sem.at[q]
+        rows = pl.ds(q * (pool_ref.shape[0] // PIECES), pool_ref.shape[0] // PIECES)
+        return pltpu.make_async_copy(pool_ref.at[rows], pool_buf.at[rows], pool_sem.at[q])
+
+    small = [
+        pltpu.make_async_copy(src, dst, small_sem.at[i])
+        for i, (src, dst) in enumerate(
+            [(assign_hbm, assign_ref), (sample_hbm, sample_ref), (counts_hbm, counts_ref), (old_hbm, old_ref)]
         )
-
-    for q in range(STEPS):
+    ]
+    for copy in small:
+        copy.start()
+    for q in range(PIECES):
         pool_copy(q).start()
     own_inverse = pltpu.make_async_copy(precond_ref.at[group], inverse.at[0], own_sem)
     own_inverse.start()
@@ -101,6 +112,7 @@
         )
 
     first = centre * SIDE
+    small[0].wait()
     assign = assign_ref[...]
     masks = [(assign == first + k) for k in range(SIDE)]
     mask_all = jnp.concatenate([m.astype(jnp.float32) for m in masks], axis=0).astype(jnp.bfloat16)
@@ -119,6 +131,7 @@
         slot_of[k * span : (k + 1) * span, :] = jnp.where(masks[k], rank[k * span : (k + 1) * span, :], -1)
     named = [jnp.sum(totals[k * span : (k + 1) * span, :], axis=0, keepdims=True) for k in range(SIDE)]
 
+    small[1].wait()
     sample = sample_ref[...] + 1
     slot_row = iota((CAP, LANES), 0)
     for k in range(SIDE):
@@ -129,11 +142,12 @@
         index = jnp.sum(total.astype(jnp.float32), axis=1, keepdims=True).astype(jnp.int32) - 1
 
         def pick(t, carry):
-            hot = (iota((CAP, COLS), 1) + t * COLS) == index
-            picker[t, k * CAP : (k + 1) * CAP, :] = hot.astype(jnp.float32).astype(jnp.bfloat16)
+            hot = (iota((CAP, 256), 1) + t * 256) == index
+            columns = pl.ds(pl.multiple_of(t * 256, 256), 256)
+            picker[k * CAP : (k + 1) * CAP, columns] = hot.astype(jnp.float32).astype(jnp.bfloat16)
             return carry
 
-        lax.fori_loop(0, picker.shape[0], pick, 0)
+        lax.fori_loop(0, picker.shape[1] // 256, pick, 0, unroll=4)
 
     pl.semaphore_wait(barrier, SIDE * SIDE - 1 + centre_count - 1)
     inverse_copies = []
@@ -148,43 +162,21 @@
         )
         copy.start()
         inverse_copies.append(copy)
-
-    sums = []
-    row_copies = []
-    for q in range(STEPS):
+    for q in range(PIECES):
         pool_copy(q).wait()
-
-        block = jnp.zeros((SIDE * CAP, COLS), jnp.float32)
-        for t in range(picker.shape[0]):
-            block += jnp.dot(
-                picker[t], pool_buf[q, t * COLS : (t + 1) * COLS, :], preferred_element_type=jnp.float32
-            )
-        picked[q] = block.astype(jnp.bfloat16)
-        sums.append(
-            [jnp.sum(block[k * CAP : (k + 1) * CAP, :], axis=0, keepdims=True) for k in range(SIDE)]
-        )
-        for b in range(1, SIDE):
-            copy = pltpu.make_async_remote_copy(
-                src_ref=picked.at[q, pl.ds(partition(b) * CAP, CAP)],
-                dst_ref=rows_in.at[b, q],
-                send_sem=row_send.at[b, q],
-                recv_sem=row_recv.at[b, q],
-                device_id=(device(0, b), centre),
-                device_id_type=MESH,
-            )
-            copy.start()
-            row_copies.append(copy)
+    block = jnp.dot(picker[...], pool_buf[...], preferred_element_type=jnp.float32)
+    picked[...] = block.astype(jnp.bfloat16)
+    sums = [jnp.sum(block[k * CAP : (k + 1) * CAP, :], axis=0, keepdims=True) for k in range(SIDE)]
 
     tile_row = iota((CHUNKS, LANES), 0)
     half = lax.rem(place, 2)
+    small[2].wait()
+    small[3].wait()
     old = old_ref[...]
     twice = jnp.concatenate([old, old], axis=1)
     twice = jnp.where(iota(twice.shape, 1) // (LANES // 2) == half, twice, 0.0)
     for k in range(SIDE):
-        rows = []
-        for q in range(STEPS):
-            for s in range(COLS // LANES):
-                rows.append(sums[q][k][:, s * LANES : (s + 1) * LANES])
+        rows = [sums[k][:, r * LANES : (r + 1) * LANES] for r in range(CHUNKS)]
         tile = ANISO * jnp.concatenate(rows, axis=0)
         prior = counts_ref[k].astype(jnp.float32)
         tile += jnp.where(tile_row == place // 2, prior * twice[k : k + 1, :], 0.0)
@@ -202,11 +194,24 @@
                     device_id_type=MESH,
                 ).start()
 
+    row_copies = []
+    for b in range(1, SIDE):
+        copy = pltpu.make_async_remote_copy(
+            src_ref=picked.at[pl.ds(partition(b) * CAP, CAP)],
+            dst_ref=rows_in.at[b],
+            send_sem=row_send.at[b],
+            recv_sem=row_recv.at[b],
+            device_id=(device(0, b), centre),
+            device_id_type=MESH,
+        )
+        copy.start()
+        row_copies.append(copy)
+
     def own_norm(i, carry):
         rows = pl.ds(i * 32, 32)
-        total = jnp.zeros((32, COLS), jnp.float32)
-        for q in range(STEPS):
-            x = picked[q, rows, :].astype(jnp.float32)
+        total = jnp.zeros((32, LANES), jnp.float32)
+        for r in range(CHUNKS):
+            x = picked[rows, r * LANES : (r + 1) * LANES].astype(jnp.float32)
             total += x * x
         mean = jnp.sum(total, axis=1, keepdims=True) * (1.0 / D)
         inv_own[rows, :] = jnp.broadcast_to(lax.rsqrt(mean + EPSILON) / math.sqrt(D), (32, LANES))
@@ -246,24 +251,18 @@
         return tile
 
     def apply_outer(vector):
-        def step(i, carry):
-            rows = pl.ds(i * 32, 32)
+        alongs = []
+        for i in range(SIDE * CAP // 32):
             total = jnp.zeros((32, LANES), jnp.float32)
-            pieces = []
-            for r in range(CHUNKS):
-                u = unit[rows, r * LANES : (r + 1) * LANES]
-                pieces.append(u)
-                total += u * vector[r : r + 1, :]
-            along = jnp.sum(total, axis=1, keepdims=True)
-            out = []
-            for r in range(CHUNKS):
-                v = pieces[r] * along
-                out.append(carry[r] + ((v[0:8] + v[8:16]) + (v[16:24] + v[24:32])))
-            return tuple(out)
-
-        zero = tuple(jnp.zeros((8, LANES), jnp.float32) for _ in range(CHUNKS))
-        parts = lax.fori_loop(0, SIDE * CAP // 32, step, zero, unroll=4)
-        return jnp.concatenate([jnp.sum(p, axis=0, keepdims=True) for p in parts], axis=0)
+            for r in range(CHUNKS):
+                total += unit[i * 32 : (i + 1) * 32, r * LANES : (r + 1) * LANES] * vector[r : r + 1, :]
+            alongs.append(jnp.sum(total, axis=1, keepdims=True))
+        along = jnp.concatenate(alongs, axis=0)
+        rows = []
+        for r in range(CHUNKS):
+            product = unit[:, r * LANES : (r + 1) * LANES] * along
+            rows.append(jnp.sum(product, axis=0, keepdims=True))
+        return jnp.concatenate(rows, axis=0)
 
     def line_sum(turn, tile):
         line_out[turn] = tile
@@ -288,24 +287,24 @@
 
     for b in range(SIDE):
         if b:
-            for q in range(STEPS):
-                pltpu.make_async_copy(rows_in.at[b, q], rows_in.at[b, q], row_recv.at[b, q]).wait()
+            row_copies[b - 1].wait_recv()
 
         def normalise(i, carry):
             x = []
-            for q in range(STEPS):
+            for r in range(CHUNKS):
+                columns = slice(r * LANES, (r + 1) * LANES)
                 if b:
-                    x.append(rows_in[b, q, pl.ds(i * 32, 32), :].astype(jnp.float32))
+                    x.append(rows_in[b, pl.ds(i * 32, 32), columns].astype(jnp.float32))
                 else:
-                    x.append(picked[q, pl.ds(group * CAP + i * 32, 32), :].astype(jnp.float32))
-            total = jnp.zeros((32, COLS), jnp.float32)
-            for q in range(STEPS):
-                total += x[q] * x[q]
+                    x.append(picked[pl.ds(group * CAP + i * 32, 32), columns].astype(jnp.float32))
+            total = jnp.zeros((32, LANES), jnp.float32)
+            for r in range(CHUNKS):
+                total += x[r] * x[r]
             mean = jnp.sum(total, axis=1, keepdims=True) * (1.0 / D)
             inv = lax.rsqrt(mean + EPSILON) / math.sqrt(D)
-            for q in range(STEPS):
-                u = (x[q] * inv).astype(jnp.bfloat16).astype(jnp.float32)
-                unit[pl.ds(b * CAP + i * 32, 32), q * COLS : (q + 1) * COLS] = u
+            for r in range(CHUNKS):
+                u = (x[r] * inv).astype(jnp.bfloat16).astype(jnp.float32)
+                unit[pl.ds(b * CAP + i * 32, 32), r * LANES : (r + 1) * LANES] = u
             return carry
 
         lax.fori_loop(0, CAP // 32, normalise, 0)
@@ -341,7 +340,6 @@
     losses = jnp.zeros((span, LANES), jnp.float32)
     centres = jnp.zeros((SIDE, LANES), jnp.float32)
     part_row = iota((SIDE, LANES), 0)
-    span_row = iota((span, LANES), 0)
     for b in range(SIDE):
         k = lax.rem(group + SIDE - b, SIDE)
         tile = whole_out[...] if b == 0 else whole_in[b]
@@ -355,23 +353,20 @@
             rows = pl.ds(k * CAP + i * 32, 32)
             square = jnp.zeros((32, LANES), jnp.float32)
             along = jnp.zeros((32, LANES), jnp.float32)
-            for q in range(STEPS):
-                x = picked[q, rows, :].astype(jnp.float32)
-                for s in range(COLS // LANES):
-                    r = q * (COLS // LANES) + s
-                    xs = x[:, s * LANES : (s + 1) * LANES]
-                    deviation = xs - tile[r : r + 1, :]
-                    square += deviation * deviation
-                    along += deviation * xs
+            for r in range(CHUNKS):
+                x = picked[rows, r * LANES : (r + 1) * LANES].astype(jnp.float32)
+                deviation = x - tile[r : r + 1, :]
+                square += deviation * deviation
+                along += deviation * x
             along = jnp.sum(along, axis=1, keepdims=True) * inv_own[rows, 0:1]
             square = jnp.sum(square, axis=1, keepdims=True)
             columns.append((square + (ANISO - 1.0) * along * along) / (ANISO * D))
         column = jnp.concatenate(columns, axis=0)
+        table = jnp.sum(jnp.where(lane_row == lane_col, column, 0.0), axis=0, keepdims=True)
+        table = jnp.broadcast_to(table, (span, LANES))
         slots = slot_of[pl.ds(k * span, span), :]
-        for r in range(span):
-            hit = slots[r : r + 1, :] == slot_row
-            row = jnp.sum(jnp.where(hit, column, 0.0), axis=0, keepdims=True)
-            losses += jnp.where(span_row == r, row, 0.0)
+        found = jnp.take_along_axis(table, jnp.maximum(slots, 0), axis=1)
+        losses += jnp.where(slots >= 0, found, 0.0)
 
     loss_out[...] = losses
     for k in range(1, centre_count):
@@ -422,21 +417,18 @@
             jax.ShapeDtypeStruct((part_dev, D // dp_count), f32),
             jax.ShapeDtypeStruct((span, LANES), f32),
         ),
-        in_specs=[
-            vmem,
-            vmem,
-            pl.BlockSpec(memory_space=pltpu.SMEM),
-            vmem,
-            pl.BlockSpec(memory_space=pl.ANY),
-            pl.BlockSpec(memory_space=pl.ANY),
-        ],
+        in_specs=[pl.BlockSpec(memory_space=pltpu.HBM)] * 6,
         out_specs=(vmem, vmem),
         scratch_shapes=[
-            pltpu.VMEM((STEPS, pool_rows, COLS), bf16),
-            pltpu.VMEM((pool_rows // COLS, SIDE * CAP, COLS), bf16),
+            pltpu.VMEM((span, LANES), jnp.int32),
+            pltpu.VMEM((span, LANES), jnp.int32),
+            pltpu.SMEM((part_dev,), jnp.int32),
+            pltpu.VMEM((part_dev, D // dp_count), f32),
+            pltpu.VMEM((pool_rows, D), bf16),
+            pltpu.VMEM((SIDE * CAP, pool_rows), bf16),
             pltpu.VMEM((SIDE * span, LANES), jnp.int32),
-            pltpu.VMEM((STEPS, SIDE * CAP, COLS), bf16),
-            pltpu.VMEM((SIDE, STEPS, CAP, COLS), bf16),
+            pltpu.VMEM((SIDE * CAP, D), bf16),
+            pltpu.VMEM((SIDE, CAP, D), bf16),
             pltpu.VMEM((SIDE * CAP, D), f32),
             pltpu.VMEM((SIDE * CAP, LANES), f32),
             pltpu.VMEM((SIDE, D // dp_count, D), bf16),
@@ -448,12 +440,13 @@
             pltpu.VMEM((plane, CHUNKS, LANES), f32),
             pltpu.VMEM((span, LANES), f32),
             pltpu.VMEM((centre_count, span, LANES), f32),
-            dma((STEPS,)),
+            dma((4,)),
+            dma((PIECES,)),
             dma,
             dma((SIDE,)),
             dma((SIDE,)),
-            dma((SIDE, STEPS)),
-            dma((SIDE, STEPS)),
+            dma((SIDE,)),
+            dma((SIDE,)),
             dma((2,)),
             dma((2 * SWEEPS,)),
             dma((2 * SWEEPS,)),
@@ -461,7 +454,7 @@
             dma((2,)),
         ],
         compiler_params=pltpu.CompilerParams(
-            collective_id=0, has_side_effects=True, vmem_limit_bytes=48 * 1024 * 1024
+            collective_id=0, has_side_effects=True, vmem_limit_bytes=64 * 1024 * 1024 - 65536
         ),
     )(sample_idx.reshape(span, LANES), assign.reshape(span, LANES), counts, old_centres, precond, pool)
     return centres, loss.reshape(row_dev)

time: 63.8 us -> 58.1 us (0.911)
  Pallas kernels: 57.9 us -> 54.8 us
  local copies, waits for them, and re-layouts: 4.94 us -> 2.53 us
    pallas_call x1, Pallas kernels: 57.9 us -> 54.8 us  [shards(): pl.pallas_call(functools.partial(kernel, centre_count, mean_load), out_sh...]
    unnamed x12 -> x2, local copies, waits for them, and re-layouts: 4.94 us -> 2.53 us
where the time goes in v2:
time: 58.1 us; the launch traced here: 57.9 us
  Pallas kernels  54.8 us (94%)
  local copies, waits for them, and re-layouts  2.53 us (4%)
  between operations  0.64 us (1%)
    pallas_call x1, Pallas kernels, shards(): pl.pallas_call(functools.partial(kernel, centre_count, mean_load), out_sh...  54.8 us
    unnamed x2, local copies, waits for them, and re-layouts  2.53 us

profile of v2, /device:TPU:1, one launch (start us, length us, event | category | flops | bytes accessed | tf_op | source)
XLA Modules:
  0.0 57.9 jit_solution(7926094807013897327)
XLA Ops:
  0.6 54.8 %shard_map.77 = (f32[4,64]{1,0:T(4,128)}, f32[16,128]{1,0:T(8,128)}) custom-call(s32[16,128]{1,0:T(8,128)} %bitcast.3, s32[16,128]{1,0:T(8,128)} %bitcast.4, s32[4]{0:T(128)} %counts_hbm.1, f32[4,64]{1,0:T(4,128)} %old_hbm.1, bf16[4,64,1024]{2,1,0:T(8,128)(2,1)} %precond_ref.1, bf16[4096,1024]{1,0:T(8,128)(2,1)} %pool_ref.1), custom_call_target="tpu_custom_call" | custom-call | tf_op jit(solution)/shard_map/pallas_call | solution.py:414
  55.4 1.2 %copy.10 = f32[4,64]{1,0:T(4,128)} copy(f32[4,64]{1,0:T(4,128)} %get-tuple-element.8) | data formatting | bytes 2048
  56.7 1.3 %copy.11 = f32[2048]{0:T(1024)} copy(f32[2048]{0:T(1024)} %bitcast.5) | data formatting | bytes 16384

commit v3 on v2

--- a/solution.py
+++ b/solution.py
@@ -19,6 +19,7 @@
 CHUNKS = D // LANES
 SIDE = 4
 PIECES = 8
+HALF = D // 2
 MESH = pl.DeviceIdType.MESH
 
 
@@ -43,6 +44,7 @@
     old_ref,
     pool_buf,
     picker,
+    times,
     slot_of,
     picked,
     rows_in,
@@ -128,23 +130,26 @@
     ahead = jnp.dot(before, totals.astype(jnp.bfloat16), preferred_element_type=jnp.float32)
     rank = (inside + ahead).astype(jnp.int32) - 1
     for k in range(SIDE):
-        slot_of[k * span : (k + 1) * span, :] = jnp.where(masks[k], rank[k * span : (k + 1) * span, :], -1)
+        slot_of[k] = jnp.where(masks[k], rank[k * span : (k + 1) * span, :], -1)
     named = [jnp.sum(totals[k * span : (k + 1) * span, :], axis=0, keepdims=True) for k in range(SIDE)]
 
     small[1].wait()
     sample = sample_ref[...] + 1
     slot_row = iota((CAP, LANES), 0)
+    times[...] = jnp.zeros(times.shape, jnp.float32)
     for k in range(SIDE):
         total = jnp.zeros((CAP, LANES), jnp.int32)
         for r in range(span):
-            hit = slot_of[k * span + r : k * span + r + 1, :] == slot_row
+            hit = slot_of[k, r : r + 1, :] == slot_row
             total += jnp.where(hit, sample[r : r + 1, :], 0)
         index = jnp.sum(total.astype(jnp.float32), axis=1, keepdims=True).astype(jnp.int32) - 1
 
         def pick(t, carry):
             hot = (iota((CAP, 256), 1) + t * 256) == index
             columns = pl.ds(pl.multiple_of(t * 256, 256), 256)
-            picker[k * CAP : (k + 1) * CAP, columns] = hot.astype(jnp.float32).astype(jnp.bfloat16)
+            hot = hot.astype(jnp.float32)
+            picker[k * CAP : (k + 1) * CAP, columns] = hot.astype(jnp.bfloat16)
+            times[k : k + 1, columns] = jnp.sum(hot, axis=0, keepdims=True)
             return carry
 
         lax.fori_loop(0, picker.shape[1] // 256, pick, 0, unroll=4)
@@ -164,19 +169,16 @@
         inverse_copies.append(copy)
     for q in range(PIECES):
         pool_copy(q).wait()
-    block = jnp.dot(picker[...], pool_buf[...], preferred_element_type=jnp.float32)
-    picked[...] = block.astype(jnp.bfloat16)
-    sums = [jnp.sum(block[k * CAP : (k + 1) * CAP, :], axis=0, keepdims=True) for k in range(SIDE)]
-
     tile_row = iota((CHUNKS, LANES), 0)
     half = lax.rem(place, 2)
     small[2].wait()
     small[3].wait()
     old = old_ref[...]
+    sums = jnp.dot(times[...].astype(jnp.bfloat16), pool_buf[...], preferred_element_type=jnp.float32)
     twice = jnp.concatenate([old, old], axis=1)
     twice = jnp.where(iota(twice.shape, 1) // (LANES // 2) == half, twice, 0.0)
     for k in range(SIDE):
-        rows = [sums[k][:, r * LANES : (r + 1) * LANES] for r in range(CHUNKS)]
+        rows = [sums[k : k + 1, r * LANES : (r + 1) * LANES] for r in range(CHUNKS)]
         tile = ANISO * jnp.concatenate(rows, axis=0)
         prior = counts_ref[k].astype(jnp.float32)
         tile += jnp.where(tile_row == place // 2, prior * twice[k : k + 1, :], 0.0)
@@ -195,29 +197,37 @@
                 ).start()
 
     row_copies = []
-    for b in range(1, SIDE):
-        copy = pltpu.make_async_remote_copy(
-            src_ref=picked.at[pl.ds(partition(b) * CAP, CAP)],
-            dst_ref=rows_in.at[b],
-            send_sem=row_send.at[b],
-            recv_sem=row_recv.at[b],
-            device_id=(device(0, b), centre),
-            device_id_type=MESH,
-        )
-        copy.start()
-        row_copies.append(copy)
-
-    def own_norm(i, carry):
-        rows = pl.ds(i * 32, 32)
-        total = jnp.zeros((32, LANES), jnp.float32)
-        for r in range(CHUNKS):
-            x = picked[rows, r * LANES : (r + 1) * LANES].astype(jnp.float32)
-            total += x * x
-        mean = jnp.sum(total, axis=1, keepdims=True) * (1.0 / D)
-        inv_own[rows, :] = jnp.broadcast_to(lax.rsqrt(mean + EPSILON) / math.sqrt(D), (32, LANES))
+    for h in range(2):
+        block = jnp.dot(picker[...], pool_buf[:, h * HALF : (h + 1) * HALF], preferred_element_type=jnp.float32)
+        picked[h] = block.astype(jnp.bfloat16).reshape(SIDE, CAP, HALF)
+        for b in range(1, SIDE):
+            copy = pltpu.make_async_remote_copy(
+                src_ref=picked.at[h, partition(b)],
+                dst_ref=rows_in.at[h, b],
+                send_sem=row_send.at[h, b],
+                recv_sem=row_recv.at[h, b],
+                device_id=(device(0, b), centre),
+                device_id_type=MESH,
+            )
+            copy.start()
+            row_copies.append(copy)
+
+    def piece(ref, part, rows, r):
+        start = r % (CHUNKS // 2) * LANES
+        return ref[r // (CHUNKS // 2), part, rows, start : start + LANES].astype(jnp.float32)
+
+    def own_norm(k, carry):
+        for i in range(CAP // 32):
+            rows = slice(i * 32, (i + 1) * 32)
+            total = jnp.zeros((32, LANES), jnp.float32)
+            for r in range(CHUNKS):
+                x = piece(picked, k, rows, r)
+                total += x * x
+            mean = jnp.sum(total, axis=1, keepdims=True) * (1.0 / D)
+            inv_own[k, rows, :] = jnp.broadcast_to(lax.rsqrt(mean + EPSILON) / math.sqrt(D), (32, LANES))
         return carry
 
-    lax.fori_loop(0, SIDE * CAP // 32, own_norm, 0)
+    lax.fori_loop(0, SIDE, own_norm, 0)
 
     own_inverse.wait()
     for copy in inverse_copies:
@@ -288,15 +298,13 @@
     for b in range(SIDE):
         if b:
             row_copies[b - 1].wait_recv()
-
-        def normalise(i, carry):
+            row_copies[b + SIDE - 2].wait_recv()
+
+        for i in range(CAP // 32):
+            rows = slice(i * 32, (i + 1) * 32)
             x = []
             for r in range(CHUNKS):
-                columns = slice(r * LANES, (r + 1) * LANES)
-                if b:
-                    x.append(rows_in[b, pl.ds(i * 32, 32), columns].astype(jnp.float32))
-                else:
-                    x.append(picked[pl.ds(group * CAP + i * 32, 32), columns].astype(jnp.float32))
+                x.append(piece(rows_in, b, rows, r) if b else piece(picked, group, rows, r))
             total = jnp.zeros((32, LANES), jnp.float32)
             for r in range(CHUNKS):
                 total += x[r] * x[r]
@@ -304,10 +312,7 @@
             inv = lax.rsqrt(mean + EPSILON) / math.sqrt(D)
             for r in range(CHUNKS):
                 u = (x[r] * inv).astype(jnp.bfloat16).astype(jnp.float32)
-                unit[pl.ds(b * CAP + i * 32, 32), r * LANES : (r + 1) * LANES] = u
-            return carry
-
-        lax.fori_loop(0, CAP // 32, normalise, 0)
+                unit[b * CAP + i * 32 : b * CAP + (i + 1) * 32, r * LANES : (r + 1) * LANES] = u
 
     vector = finish()
     for sweep in range(SWEEPS):
@@ -350,21 +355,21 @@
 
         columns = []
         for i in range(CAP // 32):
-            rows = pl.ds(k * CAP + i * 32, 32)
+            rows = slice(i * 32, (i + 1) * 32)
             square = jnp.zeros((32, LANES), jnp.float32)
             along = jnp.zeros((32, LANES), jnp.float32)
             for r in range(CHUNKS):
-                x = picked[rows, r * LANES : (r + 1) * LANES].astype(jnp.float32)
+                x = piece(picked, k, rows, r)
                 deviation = x - tile[r : r + 1, :]
                 square += deviation * deviation
                 along += deviation * x
-            along = jnp.sum(along, axis=1, keepdims=True) * inv_own[rows, 0:1]
+            along = jnp.sum(along, axis=1, keepdims=True) * inv_own[k, rows, 0:1]
             square = jnp.sum(square, axis=1, keepdims=True)
             columns.append((square + (ANISO - 1.0) * along * along) / (ANISO * D))
         column = jnp.concatenate(columns, axis=0)
         table = jnp.sum(jnp.where(lane_row == lane_col, column, 0.0), axis=0, keepdims=True)
         table = jnp.broadcast_to(table, (span, LANES))
-        slots = slot_of[pl.ds(k * span, span), :]
+        slots = slot_of[k]
         found = jnp.take_along_axis(table, jnp.maximum(slots, 0), axis=1)
         losses += jnp.where(slots >= 0, found, 0.0)
 
@@ -426,11 +431,12 @@
             pltpu.VMEM((part_dev, D // dp_count), f32),
             pltpu.VMEM((pool_rows, D), bf16),
             pltpu.VMEM((SIDE * CAP, pool_rows), bf16),
-            pltpu.VMEM((SIDE * span, LANES), jnp.int32),
-            pltpu.VMEM((SIDE * CAP, D), bf16),
-            pltpu.VMEM((SIDE, CAP, D), bf16),
+            pltpu.VMEM((8, pool_rows), f32),
+            pltpu.VMEM((SIDE, span, LANES), jnp.int32),
+            pltpu.VMEM((2, SIDE, CAP, HALF), bf16),
+            pltpu.VMEM((2, SIDE, CAP, HALF), bf16),
             pltpu.VMEM((SIDE * CAP, D), f32),
-            pltpu.VMEM((SIDE * CAP, LANES), f32),
+            pltpu.VMEM((SIDE, CAP, LANES), f32),
             pltpu.VMEM((SIDE, D // dp_count, D), bf16),
             pltpu.VMEM((SIDE, 2, CHUNKS, LANES), f32),
             pltpu.VMEM((plane, 2, CHUNKS, LANES), f32),
@@ -445,8 +451,8 @@
             dma,
             dma((SIDE,)),
             dma((SIDE,)),
-            dma((SIDE,)),
-            dma((SIDE,)),
+            dma((2, SIDE)),
+            dma((2, SIDE)),
             dma((2,)),
             dma((2 * SWEEPS,)),
             dma((2 * SWEEPS,)),
@@ -454,9 +460,9 @@
             dma((2,)),
         ],
         compiler_params=pltpu.CompilerParams(
-            collective_id=0, has_side_effects=True, vmem_limit_bytes=64 * 1024 * 1024 - 65536
+            collective_id=0, has_side_effects=True, vmem_limit_bytes=48 * 1024 * 1024
         ),
-    )(sample_idx.reshape(span, LANES), assign.reshape(span, LANES), counts, old_centres, precond, pool)
+    )(*(pltpu.with_memory_space_constraint(a, pltpu.HBM) for a in (sample_idx.reshape(span, LANES), assign.reshape(span, LANES), counts, old_centres, precond, pool)))
     return centres, loss.reshape(row_dev)
 
 

time: 58.1 us -> 54 us (0.929)
  Pallas kernels: 54.8 us -> 52.1 us
  local copies, waits for them, and re-layouts: 2.53 us -> 1.18 us
    pallas_call x1, Pallas kernels: 54.8 us -> 52.1 us  [shards(): pl.pallas_call(functools.partial(kernel, centre_count, mean_load), out_sh...]
    unnamed x2, local copies, waits for them, and re-layouts: 2.53 us -> 1.18 us
where the time goes in v3:
time: 54 us; the launch traced here: 53.9 us
  Pallas kernels  52.1 us (96%)
  local copies, waits for them, and re-layouts  1.18 us (2%)
  between operations  0.64 us (1%)
    pallas_call x1, Pallas kernels, shards(): pl.pallas_call(functools.partial(kernel, centre_count, mean_load), out_sh...  52.1 us
    unnamed x2, local copies, waits for them, and re-layouts  1.18 us

profile of v3, /device:TPU:1, one launch (start us, length us, event | category | flops | bytes accessed | tf_op | source)
XLA Modules:
  0.0 53.9 jit_solution(6498962280393143095)
XLA Ops:
  0.6 52.1 %shard_map.77 = (f32[4,64]{1,0:T(4,128)S(1)}, f32[16,128]{1,0:T(8,128)S(1)}) custom-call(s32[16,128]{1,0:T(8,128)} %bitcast.4, s32[16,128]{1,0:T(8,128)} %bitcast.5, s32[4]{0:T(128)} %counts_hbm.1, f32[4,64]{1,0:T(4,128)} %old_hbm.1, bf16[4,64,1024]{2,1,0:T(8,128)(2,1)} %precond_ref.1, bf16[4096,1024]{1,0:T(8,128)(2,1)} %pool_ref.1), custom_call_target="tpu_custom_call" | custom-call | tf_op jit(solution)/shard_map/pallas_call | solution.py:419
  52.7 0.6 %copy.10 = f32[4,64]{1,0:T(4,128)} copy(f32[4,64]{1,0:T(4,128)S(1)} %get-tuple-element.8) | data formatting | bytes 2048
  53.3 0.6 %copy.11 = f32[2048]{0:T(1024)} copy(f32[2048]{0:T(1024)S(1)} %bitcast.3) | data formatting | bytes 16384

commit v4 on v3

--- a/solution.py
+++ b/solution.py
@@ -21,6 +21,12 @@
 PIECES = 8
 HALF = D // 2
 MESH = pl.DeviceIdType.MESH
+
+
+FAR = sorted(
+    [(a, b) for a in range(SIDE) for b in range(SIDE) if a or b],
+    key=lambda step: -sum(min(n, SIDE - n) for n in step),
+)
 
 
 def iota(shape, axis):
@@ -53,6 +59,8 @@
     inverse,
     moment_out,
     moment_in,
+    count_out,
+    count_in,
     line_out,
     line_in,
     whole_out,
@@ -67,6 +75,8 @@
     row_send,
     row_recv,
     moment_sem,
+    count_send,
+    count_recv,
     line_send,
     line_recv,
     whole_sem,
@@ -104,10 +114,8 @@
     own_inverse.start()
 
     barrier = pltpu.get_barrier_semaphore()
-    for a in range(SIDE):
-        for b in range(SIDE):
-            if a or b:
-                pl.semaphore_signal(barrier, inc=1, device_id=(device(a, b), centre), device_id_type=MESH)
+    for a, b in FAR:
+        pl.semaphore_signal(barrier, inc=1, device_id=(device(a, b), centre), device_id_type=MESH)
     for k in range(1, centre_count):
         pl.semaphore_signal(
             barrier, inc=1, device_id=(place, lax.rem(centre + k, centre_count)), device_id_type=MESH
@@ -182,19 +190,17 @@
         tile = ANISO * jnp.concatenate(rows, axis=0)
         prior = counts_ref[k].astype(jnp.float32)
         tile += jnp.where(tile_row == place // 2, prior * twice[k : k + 1, :], 0.0)
-        moment_out[k, 0] = tile
-        moment_out[k, 1] = jnp.broadcast_to(named[k], (CHUNKS, LANES))
-    for a in range(SIDE):
-        for b in range(SIDE):
-            if a or b:
-                pltpu.make_async_remote_copy(
-                    src_ref=moment_out.at[partition(b)],
-                    dst_ref=moment_in.at[a * SIDE + b],
-                    send_sem=moment_sem.at[0],
-                    recv_sem=moment_sem.at[1],
-                    device_id=(device(a, b), centre),
-                    device_id_type=MESH,
-                ).start()
+        moment_out[k] = tile
+        count_out[k] = jnp.broadcast_to(named[k], (CHUNKS, LANES))
+    for a, b in FAR:
+        pltpu.make_async_remote_copy(
+            src_ref=moment_out.at[partition(b)],
+            dst_ref=moment_in.at[a * SIDE + b],
+            send_sem=moment_sem.at[0],
+            recv_sem=moment_sem.at[1],
+            device_id=(device(a, b), centre),
+            device_id_type=MESH,
+        ).start()
 
     row_copies = []
     for h in range(2):
@@ -211,6 +217,18 @@
             )
             copy.start()
             row_copies.append(copy)
+    count_copies = []
+    for b in range(1, SIDE):
+        copy = pltpu.make_async_remote_copy(
+            src_ref=count_out.at[partition(b)],
+            dst_ref=count_in.at[b],
+            send_sem=count_send.at[b],
+            recv_sem=count_recv.at[b],
+            device_id=(device(0, b), centre),
+            device_id_type=MESH,
+        )
+        copy.start()
+        count_copies.append(copy)
 
     def piece(ref, part, rows, r):
         start = r % (CHUNKS // 2) * LANES
@@ -234,15 +252,12 @@
         copy.wait_recv()
     arrived = moment_in.at[pl.ds(1, SIDE * SIDE - 1)]
     pltpu.make_async_copy(arrived, arrived, moment_sem.at[1]).wait()
-    moment = moment_out[group, 0]
-    count = moment_out[group, 1]
+    moment = moment_out[group]
     for s in range(1, SIDE * SIDE):
-        moment += moment_in[s, 0]
-        count += moment_in[s, 1]
+        moment += moment_in[s]
     prior = counts_ref[group].astype(jnp.float32)
     scale = prior + mean_load
     moment = moment / scale
-    ridge = (count + prior) / scale
 
     block_row, block_lane = iota((64, LANES), 0), iota((64, LANES), 1)
 
@@ -276,7 +291,7 @@
 
     def line_sum(turn, tile):
         line_out[turn] = tile
-        for a in range(1, SIDE):
+        for a in (2, 1, 3):
             pltpu.make_async_remote_copy(
                 src_ref=line_out.at[turn],
                 dst_ref=line_in.at[turn, a],
@@ -314,10 +329,15 @@
                 u = (x[r] * inv).astype(jnp.bfloat16).astype(jnp.float32)
                 unit[b * CAP + i * 32 : b * CAP + (i + 1) * 32, r * LANES : (r + 1) * LANES] = u
 
+    count = count_out[group]
+    for b in range(1, SIDE):
+        count_copies[b - 1].wait_recv()
+        count += count_in[b]
     vector = finish()
     for sweep in range(SWEEPS):
-        product = line_sum(2 * sweep + 1, apply_outer(vector))()
-        slack = moment - ((ANISO - 1.0) / scale * product + ridge * vector)
+        share = (ANISO - 1.0) * apply_outer(vector) + count * vector
+        product = line_sum(2 * sweep + 1, share)()
+        slack = moment - (product + prior * vector) / scale
         change = apply_inverse(slack)
         if sweep < SWEEPS - 1:
             vector = vector + line_sum(2 * sweep + 2, change)()
@@ -328,17 +348,15 @@
         home = device(0, b)
         mine += jnp.where((tile_row == home // 2) & (lane // 64 == lax.rem(home, 2)), vector, 0.0)
     whole_out[...] = mine + change
-    for a in range(SIDE):
-        for b in range(SIDE):
-            if a or b:
-                pltpu.make_async_remote_copy(
-                    src_ref=whole_out,
-                    dst_ref=whole_in.at[a * SIDE + b],
-                    send_sem=whole_sem.at[0],
-                    recv_sem=whole_sem.at[1],
-                    device_id=(device(a, b), centre),
-                    device_id_type=MESH,
-                ).start()
+    for a, b in FAR:
+        pltpu.make_async_remote_copy(
+            src_ref=whole_out,
+            dst_ref=whole_in.at[a * SIDE + b],
+            send_sem=whole_sem.at[0],
+            recv_sem=whole_sem.at[1],
+            device_id=(device(a, b), centre),
+            device_id_type=MESH,
+        ).start()
     arrived = whole_in.at[pl.ds(1, SIDE * SIDE - 1)]
     pltpu.make_async_copy(arrived, arrived, whole_sem.at[1]).wait()
 
@@ -374,7 +392,7 @@
         losses += jnp.where(slots >= 0, found, 0.0)
 
     loss_out[...] = losses
-    for k in range(1, centre_count):
+    for k in sorted(range(1, centre_count), key=lambda k: abs(2 * k - centre_count)):
         pltpu.make_async_remote_copy(
             src_ref=loss_out,
             dst_ref=loss_in.at[k],
@@ -386,7 +404,7 @@
 
     swapped = jnp.concatenate([centres[:, 64:], centres[:, :64]], axis=1)
     centres_ref[...] = jnp.where(half == 0, centres, swapped)[:, :64]
-    for copy in inverse_copies + row_copies:
+    for copy in inverse_copies + row_copies + count_copies:
         copy.wait_send()
     sent = moment_in.at[pl.ds(1, SIDE * SIDE - 1)]
     pltpu.make_async_copy(sent, sent, moment_sem.at[0]).wait()
@@ -438,8 +456,10 @@
             pltpu.VMEM((SIDE * CAP, D), f32),
             pltpu.VMEM((SIDE, CAP, LANES), f32),
             pltpu.VMEM((SIDE, D // dp_count, D), bf16),
-            pltpu.VMEM((SIDE, 2, CHUNKS, LANES), f32),
-            pltpu.VMEM((plane, 2, CHUNKS, LANES), f32),
+            pltpu.VMEM((SIDE, CHUNKS, LANES), f32),
+            pltpu.VMEM((plane, CHUNKS, LANES), f32),
+            pltpu.VMEM((SIDE, CHUNKS, LANES), f32),
+            pltpu.VMEM((SIDE, CHUNKS, LANES), f32),
             pltpu.VMEM((2 * SWEEPS, CHUNKS, LANES), f32),
             pltpu.VMEM((2 * SWEEPS, SIDE, CHUNKS, LANES), f32),
             pltpu.VMEM((CHUNKS, LANES), f32),
@@ -454,6 +474,8 @@
             dma((2, SIDE)),
             dma((2, SIDE)),
             dma((2,)),
+            dma((SIDE,)),
+            dma((SIDE,)),
             dma((2 * SWEEPS,)),
             dma((2 * SWEEPS,)),
             dma((2,)),

time: 54 us -> 52.9 us (0.980)
  Pallas kernels: 52.1 us -> 51 us
    pallas_call x1, Pallas kernels: 52.1 us -> 51 us  [shards(): pl.pallas_call(functools.partial(kernel, centre_count, mean_load), out_sh...]
where the time goes in v4:
time: 52.9 us; the launch traced here: 52.8 us
  Pallas kernels  51 us (96%)
  local copies, waits for them, and re-layouts  1.18 us (2%)
  between operations  0.64 us (1%)
    pallas_call x1, Pallas kernels, shards(): pl.pallas_call(functools.partial(kernel, centre_count, mean_load), out_sh...  51 us
    unnamed x2, local copies, waits for them, and re-layouts  1.18 us

profile of v4, /device:TPU:1, one launch (start us, length us, event | category | flops | bytes accessed | tf_op | source)
XLA Modules:
  0.0 52.8 jit_solution(2216701661330924944)
XLA Ops:
  0.6 51.0 %shard_map.77 = (f32[4,64]{1,0:T(4,128)S(1)}, f32[16,128]{1,0:T(8,128)S(1)}) custom-call(s32[16,128]{1,0:T(8,128)} %bitcast.4, s32[16,128]{1,0:T(8,128)} %bitcast.5, s32[4]{0:T(128)} %counts_hbm.1, f32[4,64]{1,0:T(4,128)} %old_hbm.1, bf16[4,64,1024]{2,1,0:T(8,128)(2,1)} %precond_ref.1, bf16[4096,1024]{1,0:T(8,128)(2,1)} %pool_ref.1), custom_call_target="tpu_custom_call" | custom-call | tf_op jit(solution)/shard_map/pallas_call | solution.py:437
  51.6 0.6 %copy.10 = f32[4,64]{1,0:T(4,128)} copy(f32[4,64]{1,0:T(4,128)S(1)} %get-tuple-element.8) | data formatting | bytes 2048
  52.2 0.6 %copy.11 = f32[2048]{0:T(1024)} copy(f32[2048]{0:T(1024)S(1)} %bitcast.3) | data formatting | bytes 16384

commit v5 on v4

--- a/solution.py
+++ b/solution.py
@@ -18,7 +18,7 @@
 LANES = 128
 CHUNKS = D // LANES
 SIDE = 4
-PIECES = 8
+PIECES = 1
 HALF = D // 2
 MESH = pl.DeviceIdType.MESH
 
@@ -164,7 +164,7 @@
 
     pl.semaphore_wait(barrier, SIDE * SIDE - 1 + centre_count - 1)
     inverse_copies = []
-    for b in range(1, SIDE):
+    for b in (2, 1, 3):
         copy = pltpu.make_async_remote_copy(
             src_ref=precond_ref.at[partition(b)],
             dst_ref=inverse.at[b],
@@ -245,8 +245,6 @@
             inv_own[k, rows, :] = jnp.broadcast_to(lax.rsqrt(mean + EPSILON) / math.sqrt(D), (32, LANES))
         return carry
 
-    lax.fori_loop(0, SIDE, own_norm, 0)
-
     own_inverse.wait()
     for copy in inverse_copies:
         copy.wait_recv()
@@ -336,7 +334,10 @@
     vector = finish()
     for sweep in range(SWEEPS):
         share = (ANISO - 1.0) * apply_outer(vector) + count * vector
-        product = line_sum(2 * sweep + 1, share)()
+        finish = line_sum(2 * sweep + 1, share)
+        if sweep == 0:
+            lax.fori_loop(0, SIDE, own_norm, 0)
+        product = finish()
         slack = moment - (product + prior * vector) / scale
         change = apply_inverse(slack)
         if sweep < SWEEPS - 1:

time: 52.9 us -> 51.7 us (0.977)
  Pallas kernels: 51 us -> 49.8 us
    pallas_call x1, Pallas kernels: 51 us -> 49.8 us  [shards(): pl.pallas_call(functools.partial(kernel, centre_count, mean_load), out_sh...]
where the time goes in v5:
time: 51.7 us; the launch traced here: 51.6 us
  Pallas kernels  49.8 us (96%)
  local copies, waits for them, and re-layouts  1.18 us (2%)
  between operations  0.64 us (1%)
    pallas_call x1, Pallas kernels, shards(): pl.pallas_call(functools.partial(kernel, centre_count, mean_load), out_sh...  49.8 us
    unnamed x2, local copies, waits for them, and re-layouts  1.18 us

profile of v5, /device:TPU:1, one launch (start us, length us, event | category | flops | bytes accessed | tf_op | source)
XLA Modules:
  0.0 51.6 jit_solution(1350302221618649224)
XLA Ops:
  0.6 49.8 %shard_map.77 = (f32[4,64]{1,0:T(4,128)S(1)}, f32[16,128]{1,0:T(8,128)S(1)}) custom-call(s32[16,128]{1,0:T(8,128)} %bitcast.4, s32[16,128]{1,0:T(8,128)} %bitcast.5, s32[4]{0:T(128)} %counts_hbm.1, f32[4,64]{1,0:T(4,128)} %old_hbm.1, bf16[4,64,1024]{2,1,0:T(8,128)(2,1)} %precond_ref.1, bf16[4096,1024]{1,0:T(8,128)(2,1)} %pool_ref.1), custom_call_target="tpu_custom_call" | custom-call | tf_op jit(solution)/shard_map/pallas_call | solution.py:438
  50.4 0.6 %copy.10 = f32[4,64]{1,0:T(4,128)} copy(f32[4,64]{1,0:T(4,128)S(1)} %get-tuple-element.8) | data formatting | bytes 2048
  51.0 0.6 %copy.11 = f32[2048]{0:T(1024)} copy(f32[2048]{0:T(1024)S(1)} %bitcast.3) | data formatting | bytes 16384

commit v6 on v5

--- a/solution.py
+++ b/solution.py
@@ -142,25 +142,27 @@
     named = [jnp.sum(totals[k * span : (k + 1) * span, :], axis=0, keepdims=True) for k in range(SIDE)]
 
     small[1].wait()
-    sample = sample_ref[...] + 1
+    sample = (sample_ref[...] + 1).astype(jnp.float32)
     slot_row = iota((CAP, LANES), 0)
     times[...] = jnp.zeros(times.shape, jnp.float32)
+    indices = []
     for k in range(SIDE):
-        total = jnp.zeros((CAP, LANES), jnp.int32)
+        total = jnp.zeros((CAP, LANES), jnp.float32)
         for r in range(span):
             hit = slot_of[k, r : r + 1, :] == slot_row
-            total += jnp.where(hit, sample[r : r + 1, :], 0)
-        index = jnp.sum(total.astype(jnp.float32), axis=1, keepdims=True).astype(jnp.int32) - 1
-
-        def pick(t, carry):
-            hot = (iota((CAP, 256), 1) + t * 256) == index
-            columns = pl.ds(pl.multiple_of(t * 256, 256), 256)
-            hot = hot.astype(jnp.float32)
+            total += jnp.where(hit, sample[r : r + 1, :], 0.0)
+        indices.append(jnp.sum(total, axis=1, keepdims=True).astype(jnp.int32) - 1)
+
+    def pick(t, carry):
+        columns = pl.ds(pl.multiple_of(t * 256, 256), 256)
+        ident = iota((CAP, 256), 1) + t * 256
+        for k in range(SIDE):
+            hot = (ident == indices[k]).astype(jnp.float32)
             picker[k * CAP : (k + 1) * CAP, columns] = hot.astype(jnp.bfloat16)
             times[k : k + 1, columns] = jnp.sum(hot, axis=0, keepdims=True)
-            return carry
-
-        lax.fori_loop(0, picker.shape[1] // 256, pick, 0, unroll=4)
+        return carry
+
+    lax.fori_loop(0, picker.shape[1] // 256, pick, 0, unroll=1)
 
     pl.semaphore_wait(barrier, SIDE * SIDE - 1 + centre_count - 1)
     inverse_copies = []
@@ -274,18 +276,19 @@
         return tile
 
     def apply_outer(vector):
-        alongs = []
+        parts = [jnp.zeros((8, LANES), jnp.float32) for _ in range(CHUNKS)]
         for i in range(SIDE * CAP // 32):
             total = jnp.zeros((32, LANES), jnp.float32)
-            for r in range(CHUNKS):
-                total += unit[i * 32 : (i + 1) * 32, r * LANES : (r + 1) * LANES] * vector[r : r + 1, :]
-            alongs.append(jnp.sum(total, axis=1, keepdims=True))
-        along = jnp.concatenate(alongs, axis=0)
-        rows = []
-        for r in range(CHUNKS):
-            product = unit[:, r * LANES : (r + 1) * LANES] * along
-            rows.append(jnp.sum(product, axis=0, keepdims=True))
-        return jnp.concatenate(rows, axis=0)
+            pieces = []
+            for r in range(CHUNKS):
+                u = unit[i * 32 : (i + 1) * 32, r * LANES : (r + 1) * LANES]
+                pieces.append(u)
+                total += u * vector[r : r + 1, :]
+            along = jnp.sum(total, axis=1, keepdims=True)
+            for r in range(CHUNKS):
+                v = pieces[r] * along
+                parts[r] += (v[0:8] + v[8:16]) + (v[16:24] + v[24:32])
+        return jnp.concatenate([jnp.sum(p, axis=0, keepdims=True) for p in parts], axis=0)
 
     def line_sum(turn, tile):
         line_out[turn] = tile

time: 51.7 us -> 51.4 us (level)
  no operation moved by 1% of the time
where the time goes in v6:
time: 51.4 us; the launch traced here: 51.3 us
  Pallas kernels  49.5 us (96%)
  local copies, waits for them, and re-layouts  1.18 us (2%)
  between operations  0.64 us (1%)
    pallas_call x1, Pallas kernels, shards(): pl.pallas_call(functools.partial(kernel, centre_count, mean_load), out_sh...  49.5 us
    unnamed x2, local copies, waits for them, and re-layouts  1.18 us

profile of v6, /device:TPU:1, one launch (start us, length us, event | category | flops | bytes accessed | tf_op | source)
XLA Modules:
  0.0 51.3 jit_solution(8419825615709827884)
XLA Ops:
  0.6 49.5 %shard_map.77 = (f32[4,64]{1,0:T(4,128)S(1)}, f32[16,128]{1,0:T(8,128)S(1)}) custom-call(s32[16,128]{1,0:T(8,128)} %bitcast.4, s32[16,128]{1,0:T(8,128)} %bitcast.5, s32[4]{0:T(128)} %counts_hbm.1, f32[4,64]{1,0:T(4,128)} %old_hbm.1, bf16[4,64,1024]{2,1,0:T(8,128)(2,1)} %precond_ref.1, bf16[4096,1024]{1,0:T(8,128)(2,1)} %pool_ref.1), custom_call_target="tpu_custom_call" | custom-call | tf_op jit(solution)/shard_map/pallas_call | solution.py:441
  50.1 0.6 %copy.10 = f32[4,64]{1,0:T(4,128)} copy(f32[4,64]{1,0:T(4,128)S(1)} %get-tuple-element.8) | data formatting | bytes 2048
  50.7 0.6 %copy.11 = f32[2048]{0:T(1024)} copy(f32[2048]{0:T(1024)S(1)} %bitcast.3) | data formatting | bytes 16384

commit v7 on v6

--- a/solution.py
+++ b/solution.py
@@ -340,17 +340,18 @@
         finish = line_sum(2 * sweep + 1, share)
         if sweep == 0:
             lax.fori_loop(0, SIDE, own_norm, 0)
+        if sweep == SWEEPS - 1:
+            lane = iota((CHUNKS, LANES), 1)
+            mine = jnp.zeros((CHUNKS, LANES), jnp.float32)
+            for b in range(SIDE):
+                home = device(0, b)
+                mine += jnp.where((tile_row == home // 2) & (lane // 64 == lax.rem(home, 2)), vector, 0.0)
         product = finish()
         slack = moment - (product + prior * vector) / scale
         change = apply_inverse(slack)
         if sweep < SWEEPS - 1:
             vector = vector + line_sum(2 * sweep + 2, change)()
 
-    lane = iota((CHUNKS, LANES), 1)
-    mine = jnp.zeros((CHUNKS, LANES), jnp.float32)
-    for b in range(SIDE):
-        home = device(0, b)
-        mine += jnp.where((tile_row == home // 2) & (lane // 64 == lax.rem(home, 2)), vector, 0.0)
     whole_out[...] = mine + change
     for a, b in FAR:
         pltpu.make_async_remote_copy(
@@ -365,15 +366,14 @@
     pltpu.make_async_copy(arrived, arrived, whole_sem.at[1]).wait()
 
     losses = jnp.zeros((span, LANES), jnp.float32)
-    centres = jnp.zeros((SIDE, LANES), jnp.float32)
+    tiles = []
     part_row = iota((SIDE, LANES), 0)
     for b in range(SIDE):
         k = lax.rem(group + SIDE - b, SIDE)
         tile = whole_out[...] if b == 0 else whole_in[b]
         for a in range(1, SIDE):
             tile = tile + whole_in[a * SIDE + b]
-        block = jnp.sum(jnp.where(tile_row == place // 2, tile, 0.0), axis=0, keepdims=True)
-        centres += jnp.where(part_row == k, block, 0.0)
+        tiles.append((k, tile))
 
         columns = []
         for i in range(CAP // 32):
@@ -406,6 +406,10 @@
             device_id_type=MESH,
         ).start()
 
+    centres = jnp.zeros((SIDE, LANES), jnp.float32)
+    for k, tile in tiles:
+        block = jnp.sum(jnp.where(tile_row == place // 2, tile, 0.0), axis=0, keepdims=True)
+        centres += jnp.where(part_row == k, block, 0.0)
     swapped = jnp.concatenate([centres[:, 64:], centres[:, :64]], axis=1)
     centres_ref[...] = jnp.where(half == 0, centres, swapped)[:, :64]
     for copy in inverse_copies + row_copies + count_copies:

time: 51.4 us -> 51.4 us (level)
  no operation moved by 1% of the time
where the time goes in v7:
time: 51.4 us; the launch traced here: 51.3 us
  Pallas kernels  49.5 us (96%)
  local copies, waits for them, and re-layouts  1.18 us (2%)
  between operations  0.64 us (1%)
    pallas_call x1, Pallas kernels, shards(): pl.pallas_call(functools.partial(kernel, centre_count, mean_load), out_sh...  49.5 us
    unnamed x2, local copies, waits for them, and re-layouts  1.18 us

profile of v7, /device:TPU:1, one launch (start us, length us, event | category | flops | bytes accessed | tf_op | source)
XLA Modules:
  0.0 51.3 jit_solution(15390329165622876166)
XLA Ops:
  0.6 49.5 %shard_map.77 = (f32[4,64]{1,0:T(4,128)S(1)}, f32[16,128]{1,0:T(8,128)S(1)}) custom-call(s32[16,128]{1,0:T(8,128)} %bitcast.4, s32[16,128]{1,0:T(8,128)} %bitcast.5, s32[4]{0:T(128)} %counts_hbm.1, f32[4,64]{1,0:T(4,128)} %old_hbm.1, bf16[4,64,1024]{2,1,0:T(8,128)(2,1)} %precond_ref.1, bf16[4096,1024]{1,0:T(8,128)(2,1)} %pool_ref.1), custom_call_target="tpu_custom_call" | custom-call | tf_op jit(solution)/shard_map/pallas_call | solution.py:445
  50.1 0.6 %copy.10 = f32[4,64]{1,0:T(4,128)} copy(f32[4,64]{1,0:T(4,128)S(1)} %get-tuple-element.8) | data formatting | bytes 2048
  50.7 0.6 %copy.11 = f32[2048]{0:T(1024)} copy(f32[2048]{0:T(1024)S(1)} %bitcast.3) | data formatting | bytes 16384
